TPU v7x, 32 devices: a whole 2x2x4 slice. The times are simulated.
32 devices in a mesh: prow: 4 (over x, core), pcol: 8 (over z, y).
Axes of the slice: x: 2, y: 2, z: 4, core: 2. Of those that a mesh axis runs over, the one named last changes fastest.
Arguments:
- blocks: bfloat16 [20480, 128, 128], P(('prow', 'pcol')), may hold values from -0.078125 to 0.078125
- row_index: int32 [20480], P(('prow', 'pcol')), may hold values from 0 to 511, as said below
- col_index: int32 [20480], P(('prow', 'pcol')), may hold values from 0 to 511, as said below
- send_tiles: int32 [512], P(('prow', 'pcol')), may hold values from 0 to 511, as said below
- lighting: bfloat16 [65536, 384], P(('prow', 'pcol')), may hold values from -6 to 6
- albedo: float32 [3, 65536], P(None, ('pcol', 'prow')), may hold values from 0.2 to 0.95
- emission: bfloat16 [65536, 384], P(('pcol', 'prow')), may hold values from -4 to 4
Outputs:
- radiance: bfloat16 [65536, 384], P(('pcol', 'prow'))
Inputs may be any that keep to these rules, and one draw needn't show every extreme that they name: `send_tiles`: group g (the blocks of device g) lists 16 distinct tiles in increasing order: exactly 4 from each of the 4 ranges of 16 block rows starting at c * 64 + r * 16, r = 0 .. 3, where c = g % 8. `row_index`: each block's row is one of its group's listed tiles, each listed tile has at least one block, and a group's blocks are ordered by row; counts per tile are uneven. `col_index`: the blocks of group g have columns in (g // 8) * 128 to (g // 8 + 1) * 128 - 1; a pair of row and column may repeat, and then the blocks add.
All inputs are finite; a program needn't handle non-finite values.
Results may differ from a plain program's by a relative error of at most 0.008.
Values may be sent and summed in bfloat16 or wider, within the bound.
A program may use at most 192 MiB of HBM per device.

v0:
```python
import math
import jax
import jax.numpy as jnp
from jax import lax
from jax.sharding import PartitionSpec as P


def per_device(blocks, row_index, col_index, send_tiles, lighting, albedo, emission):
    tile_size = blocks.shape[1]
    col_width = lighting.shape[1]
    block_count = blocks.shape[0]
    list_count = send_tiles.shape[0]
    prow_count = lax.axis_size("prow")
    own_count = emission.shape[0] // tile_size
    strip_rows = own_count * prow_count
    prow_here = lax.axis_index("prow")
    pcol_here = lax.axis_index("pcol")
    slab = lax.all_gather(lighting, "pcol", axis=0, tiled=True)
    slab_count = slab.shape[0] // tile_size
    slab_flat = slab.reshape(slab_count, tile_size * col_width)
    local_cols = col_index - prow_here * slab_count
    slots = jnp.sum((send_tiles[None, :] < row_index[:, None]).astype(jnp.int32), axis=1)
    group_size = math.gcd(block_count, 64)
    group_total = block_count // group_size
    list_iota = jnp.arange(list_count, dtype=jnp.int32)

    def one_group(running, items):
        block_set, col_set, slot_set = items
        picked = jnp.take(slab_flat, col_set, axis=0).reshape(group_size, tile_size, col_width)
        product = jnp.einsum("gpq,gqk->gpk", block_set, picked, preferred_element_type=jnp.float32)
        placing = (list_iota[:, None] == slot_set[None, :]).astype(jnp.float32)
        summed_here = jnp.dot(
            placing,
            product.reshape(group_size, tile_size * col_width),
            precision=lax.Precision.HIGHEST,
            preferred_element_type=jnp.float32,
        )
        return (running + summed_here, None)

    start = jnp.zeros((list_count, tile_size * col_width), jnp.float32)
    summed, _ = lax.scan(
        one_group,
        start,
        (
            blocks.reshape(group_total, group_size, tile_size, tile_size),
            local_cols.reshape(group_total, group_size),
            slots.reshape(group_total, group_size),
        ),
    )
    part = summed.reshape(list_count, tile_size, col_width).astype(jnp.bfloat16)
    per_owner = list_count // prow_count
    arrived, arrived_ids = (
        lax.all_to_all(
            part.reshape(prow_count, per_owner, tile_size, col_width),
            "prow",
            split_axis=0,
            concat_axis=0,
            tiled=True,
        ),
        lax.all_to_all(
            send_tiles.reshape(prow_count, per_owner),
            "prow",
            split_axis=0,
            concat_axis=0,
            tiled=True,
        ),
    )
    owned_ids = arrived_ids.reshape(-1) - (pcol_here * strip_rows + prow_here * own_count)
    placing = (jnp.arange(own_count)[:, None] == owned_ids[None, :]).astype(jnp.bfloat16)
    gathered = jnp.einsum(
        "os,spk->opk",
        placing,
        arrived.reshape(list_count, tile_size, col_width),
        preferred_element_type=jnp.float32,
    )
    patch_count = own_count * tile_size
    colour_count = albedo.shape[0]
    lit = (
        gathered.reshape(patch_count, colour_count, col_width // colour_count)
        * jnp.transpose(albedo)[:, :, None]
    )
    return (lit.reshape(patch_count, col_width) + emission.astype(jnp.float32)).astype(jnp.bfloat16)


def solution(mesh):
    placed = (
        P(("prow", "pcol"), None, None),
        P(("prow", "pcol")),
        P(("prow", "pcol")),
        P(("prow", "pcol")),
        P(("prow", "pcol"), None),
        P(None, ("pcol", "prow")),
        P(("pcol", "prow"), None),
    )
    return jax.shard_map(
        per_device, mesh=mesh, in_specs=placed, out_specs=P(("pcol", "prow"), None), check_vma=False
    )
```

profile of v0, /device:TPU:0, one launch (start us, length us, event | category | flops | bytes accessed | tf_op | source)
XLA Modules:
  0.0 805.6 jit_solution(11871469207304912627)
XLA Ops:
  14.4 174.3 %all-gather.2.cloned.1.call-done = bf16[16384,384]{1,0:T(8,128)(2,1)} async-done(((bf16[2048,384]{1,0:T(8,128)(2,1)}), bf16[16384,384]{1,0:T(8,128)(2,1)}) %all-gather.2.cloned.1.call-update) | async-done | bytes 12582928 | tf_op jit(solution)/shard_map/all_gather | solution.py:18
  188.7 17.2 %reshape.88 = bf16[128,49152]{1,0:T(8,128)(2,1)} reshape(bf16[16384,384]{1,0:T(8,128)(2,1)} %all-gather.2.cloned.1.call-done) | data formatting | bytes 25165824 | tf_op jit(solution)/shard_map/reshape | solution.py:20
  205.9 558.7 %while.11 = (s32[]{:T(128)}, f32[16,49152]{1,0:T(8,128)S(1)}, s32[10,64]{1,0:T(8,128)S(1)}, bf16[10,64,128,128]{3,2,1,0:T(8,128)(2,1)}, s32[10,64]{1,0:T(8,128)S...) while((s32[]{:T(128)}, f32[16,49152]{1,0:T(8,128)S(1)}, s32[10,64]{1,0:T(8,128)S(1)}, ...), condition=%wide.region_2.3_spmd.clone, body=%wide.region_1.2_spmd.clone.sunk | while | flops 1414007296 | bytes 102767336 | solution.py:41
  205.9 18.6 %gather_fusion = bf16[64,49152]{1,0:T(8,128)(2,1)} fusion(bf16[128,49152]{1,0:T(8,128)(2,1)} %get-tuple-element.136, s32[1024]{0:T(1024)S(1)} %pad_clamp_fusion.2), kind=kCustom, calls=%fused_computation.clone.clone.1 | custom fusion | bytes 12583168 | tf_op jit(solution)/shard_map/while/body/eval_jaxpr/jit(_take)/gather | solution.py:29
  238.1 16.3 %copy.33 = f32[8,8,128,384]{3,1,2,0:T(8,128)} copy(f32[8,8,128,384]{3,2,1,0:T(8,128)} %bitcast.59) | data formatting | bytes 25165824 | tf_op jit(solution)/shard_map/while
  261.8 18.6 %gather_fusion = bf16[64,49152]{1,0:T(8,128)(2,1)} fusion(bf16[128,49152]{1,0:T(8,128)(2,1)} %get-tuple-element.136, s32[1024]{0:T(1024)S(1)} %pad_clamp_fusion.2), kind=kCustom, calls=%fused_computation.clone.clone.1 | custom fusion | bytes 12583168 | tf_op jit(solution)/shard_map/while/body/eval_jaxpr/jit(_take)/gather | solution.py:29
  293.9 16.3 %copy.33 = f32[8,8,128,384]{3,1,2,0:T(8,128)} copy(f32[8,8,128,384]{3,2,1,0:T(8,128)} %bitcast.59) | data formatting | bytes 25165824 | tf_op jit(solution)/shard_map/while
  317.6 18.6 %gather_fusion = bf16[64,49152]{1,0:T(8,128)(2,1)} fusion(bf16[128,49152]{1,0:T(8,128)(2,1)} %get-tuple-element.136, s32[1024]{0:T(1024)S(1)} %pad_clamp_fusion.2), kind=kCustom, calls=%fused_computation.clone.clone.1 | custom fusion | bytes 12583168 | tf_op jit(solution)/shard_map/while/body/eval_jaxpr/jit(_take)/gather | solution.py:29
  349.8 16.3 %copy.33 = f32[8,8,128,384]{3,1,2,0:T(8,128)} copy(f32[8,8,128,384]{3,2,1,0:T(8,128)} %bitcast.59) | data formatting | bytes 25165824 | tf_op jit(solution)/shard_map/while
  373.5 18.6 %gather_fusion = bf16[64,49152]{1,0:T(8,128)(2,1)} fusion(bf16[128,49152]{1,0:T(8,128)(2,1)} %get-tuple-element.136, s32[1024]{0:T(1024)S(1)} %pad_clamp_fusion.2), kind=kCustom, calls=%fused_computation.clone.clone.1 | custom fusion | bytes 12583168 | tf_op jit(solution)/shard_map/while/body/eval_jaxpr/jit(_take)/gather | solution.py:29
  405.6 16.3 %copy.33 = f32[8,8,128,384]{3,1,2,0:T(8,128)} copy(f32[8,8,128,384]{3,2,1,0:T(8,128)} %bitcast.59) | data formatting | bytes 25165824 | tf_op jit(solution)/shard_map/while
  429.3 18.6 %gather_fusion = bf16[64,49152]{1,0:T(8,128)(2,1)} fusion(bf16[128,49152]{1,0:T(8,128)(2,1)} %get-tuple-element.136, s32[1024]{0:T(1024)S(1)} %pad_clamp_fusion.2), kind=kCustom, calls=%fused_computation.clone.clone.1 | custom fusion | bytes 12583168 | tf_op jit(solution)/shard_map/while/body/eval_jaxpr/jit(_take)/gather | solution.py:29
  461.5 16.3 %copy.33 = f32[8,8,128,384]{3,1,2,0:T(8,128)} copy(f32[8,8,128,384]{3,2,1,0:T(8,128)} %bitcast.59) | data formatting | bytes 25165824 | tf_op jit(solution)/shard_map/while
  485.2 18.6 %gather_fusion = bf16[64,49152]{1,0:T(8,128)(2,1)} fusion(bf16[128,49152]{1,0:T(8,128)(2,1)} %get-tuple-element.136, s32[1024]{0:T(1024)S(1)} %pad_clamp_fusion.2), kind=kCustom, calls=%fused_computation.clone.clone.1 | custom fusion | bytes 12583168 | tf_op jit(solution)/shard_map/while/body/eval_jaxpr/jit(_take)/gather | solution.py:29
  517.3 16.3 %copy.33 = f32[8,8,128,384]{3,1,2,0:T(8,128)} copy(f32[8,8,128,384]{3,2,1,0:T(8,128)} %bitcast.59) | data formatting | bytes 25165824 | tf_op jit(solution)/shard_map/while
  541.0 18.6 %gather_fusion = bf16[64,49152]{1,0:T(8,128)(2,1)} fusion(bf16[128,49152]{1,0:T(8,128)(2,1)} %get-tuple-element.136, s32[1024]{0:T(1024)S(1)} %pad_clamp_fusion.2), kind=kCustom, calls=%fused_computation.clone.clone.1 | custom fusion | bytes 12583168 | tf_op jit(solution)/shard_map/while/body/eval_jaxpr/jit(_take)/gather | solution.py:29
  573.2 16.3 %copy.33 = f32[8,8,128,384]{3,1,2,0:T(8,128)} copy(f32[8,8,128,384]{3,2,1,0:T(8,128)} %bitcast.59) | data formatting | bytes 25165824 | tf_op jit(solution)/shard_map/while
  596.9 18.6 %gather_fusion = bf16[64,49152]{1,0:T(8,128)(2,1)} fusion(bf16[128,49152]{1,0:T(8,128)(2,1)} %get-tuple-element.136, s32[1024]{0:T(1024)S(1)} %pad_clamp_fusion.2), kind=kCustom, calls=%fused_computation.clone.clone.1 | custom fusion | bytes 12583168 | tf_op jit(solution)/shard_map/while/body/eval_jaxpr/jit(_take)/gather | solution.py:29
  629.0 16.3 %copy.33 = f32[8,8,128,384]{3,1,2,0:T(8,128)} copy(f32[8,8,128,384]{3,2,1,0:T(8,128)} %bitcast.59) | data formatting | bytes 25165824 | tf_op jit(solution)/shard_map/while
  652.7 18.6 %gather_fusion = bf16[64,49152]{1,0:T(8,128)(2,1)} fusion(bf16[128,49152]{1,0:T(8,128)(2,1)} %get-tuple-element.136, s32[1024]{0:T(1024)S(1)} %pad_clamp_fusion.2), kind=kCustom, calls=%fused_computation.clone.clone.1 | custom fusion | bytes 12583168 | tf_op jit(solution)/shard_map/while/body/eval_jaxpr/jit(_take)/gather | solution.py:29
  684.9 16.3 %copy.33 = f32[8,8,128,384]{3,1,2,0:T(8,128)} copy(f32[8,8,128,384]{3,2,1,0:T(8,128)} %bitcast.59) | data formatting | bytes 25165824 | tf_op jit(solution)/shard_map/while
  708.6 18.6 %gather_fusion = bf16[64,49152]{1,0:T(8,128)(2,1)} fusion(bf16[128,49152]{1,0:T(8,128)(2,1)} %get-tuple-element.136, s32[1024]{0:T(1024)S(1)} %pad_clamp_fusion.2), kind=kCustom, calls=%fused_computation.clone.clone.1 | custom fusion | bytes 12583168 | tf_op jit(solution)/shard_map/while/body/eval_jaxpr/jit(_take)/gather | solution.py:29
  740.7 16.3 %copy.33 = f32[8,8,128,384]{3,1,2,0:T(8,128)} copy(f32[8,8,128,384]{3,2,1,0:T(8,128)} %bitcast.59) | data formatting | bytes 25165824 | tf_op jit(solution)/shard_map/while
  775.2 16.6 %all-to-all-done.1 = bf16[4,4,128,384]{3,1,2,0:T(4,128)(2,1)} async-done(((bf16[4,4,128,384]{3,1,2,0:T(4,128)(2,1)}), bf16[4,4,128,384]{3,1,2,0:T(4,128)(2,1)}, u32[]{:S(2)}, u32[]{:S(2)}) %all-to-all-start.1) | async-done | bytes 1572896 | tf_op jit(solution)/shard_map/all_to_all | solution.py:53
  (109 shorter events, 234.2 us)
Async XLA Ops:
  6.5 182.2 %all-gather.2.cloned.1.call-start = ((), (), s32[]{:S(2)}) async-start(), calls=%async_computation.2 | async-start | bytes 14155776 | tf_op jit(solution)/shard_map/all_gather | solution.py:18
  8.6 758.8 %all-to-all-start = ((s32[4,1,4]{2,1,0:T(1,128)}), s32[4,1,4]{2,1,0:T(1,128)}, u32[]{:S(2)}, u32[]{:S(2)}) async-start(s32[4,1,4]{2,1,0:T(1,128)} %bitcast), calls=%async_computation | async-start | bytes 4096 | tf_op jit(solution)/shard_map/all_to_all | solution.py:60
  765.0 6.7 copy-start.2
  767.4 24.5 %all-to-all-start.1 = ((bf16[4,4,128,384]{3,1,2,0:T(4,128)(2,1)}), bf16[4,4,128,384]{3,1,2,0:T(4,128)(2,1)}, u32[]{:S(2)}, u32[]{:S(2)}) async-start(bf16[4,4,128,384]{3,1,2,0:T(4,128)(2,1)} %copy.23), calls=%async_computation.1 | async-start | bytes 3145728 | tf_op jit(solution)/shard_map/all_to_all | solution.py:53
  794.8 1.9 copy-start
  794.8 2.3 copy-start.1
Sparse Core Ops, SparseCore 0:
  9.5 179.1 all-gather.1
where the time goes:
time: 808 us; the launch traced here: 806 us
  local copies, waits for them, and re-layouts  420 us (52%)
  waiting for transfers between devices  192 us (24%)
  matrix products  154 us (19%)
  other arithmetic  17.8 us (2%)
  between operations  13.5 us (2%)
  starting transfers between devices  8.55 us (1%)
    while x20, local copies, waits for them, and re-layouts  204 us
    gather x10, local copies, waits for them, and re-layouts, one_group(): jnp.take(slab_flat, col_set, axis=0)  186 us
    all_gather x1, waiting for transfers between devices, per_device(): slab = lax.all_gather(lighting, 'pcol', axis=0, tiled=True)  174 us
    dot_general x10, matrix products, one_group(): jnp.einsum('gpq,gqk->gpk', block_set, picked, preferred_element_type=jnp....  79 us
    dot_general x10, matrix products, one_group(): jnp.dot(placing, product.reshape(group_size, tile_size * col_width), prec...  74.1 us
    reshape x1, local copies, waits for them, and re-layouts, per_device(): slab_flat = slab.reshape(slab_count, tile_size * col_width)  17.2 us
    all_to_all x1, waiting for transfers between devices, per_device(): lax.all_to_all(part.reshape(prow_count, per_owner, tile_size, col_width),...  16.6 us
  transfers between devices with their start and end apart: 3, of which 2 were waited for; matrix products, arithmetic and copies ran while one was open for 72% of the time, Pallas kernels for 0%

commit v1 on v0

--- a/solution.py
+++ b/solution.py
@@ -3,6 +3,37 @@
 import jax.numpy as jnp
 from jax import lax
 from jax.sharding import PartitionSpec as P
+from jax.lax import axis_index, axis_size, ppermute
+
+
+def squares_render(z_in, dim_at):
+    outcome_arr = list(z_in.shape[1:])
+    outcome_arr[dim_at] *= z_in.shape[0]
+    return jnp.moveaxis(z_in, 0, dim_at).reshape(outcome_arr)
+
+
+def target_pass(field, device_axis, join_dim=0):
+    p_count = axis_size(device_axis)
+    pages = [(ix, (ix + 1) % p_count) for ix in range(p_count)]
+    current_block, everything = ([], [])
+    sheets = [(hop_no, pp) for pp, hop_no in pages]
+    for p in range(p_count - 1):
+        if p % 2 == 0:
+            current_block.append(
+                ppermute(
+                    current_block[-1] if current_block else field, axis_name=device_axis, perm=pages
+                )
+            )
+        else:
+            everything.append(
+                ppermute(
+                    everything[-1] if everything else field, axis_name=device_axis, perm=sheets
+                )
+            )
+    plain = jnp.stack([*current_block[::-1], field, *everything])
+    newest = axis_index(device_axis) - len(current_block)
+    plain = plain[(jnp.arange(p_count) - newest) % p_count]
+    return squares_render(plain, join_dim)
 
 
 def per_device(blocks, row_index, col_index, send_tiles, lighting, albedo, emission):
@@ -15,7 +46,7 @@
     strip_rows = own_count * prow_count
     prow_here = lax.axis_index("prow")
     pcol_here = lax.axis_index("pcol")
-    slab = lax.all_gather(lighting, "pcol", axis=0, tiled=True)
+    slab = target_pass(lighting, "pcol")
     slab_count = slab.shape[0] // tile_size
     slab_flat = slab.reshape(slab_count, tile_size * col_width)
     local_cols = col_index - prow_here * slab_count

time: 808 us -> 887 us (1.098)
  waiting for transfers between devices: 192 us -> 238 us
  local copies, waits for them, and re-layouts: 420 us -> 449 us
  starting transfers between devices: 8.55 us -> 25.2 us
  between operations: 13.5 us -> 0.17 us
    ppermute x0 -> x7, waiting for transfers between devices: none -> 222 us  [the longest x4 222 us: target_pass(): ppermute(current_block[-1] if current_block else field, axis_name=device_...]
    all_gather x1 -> x0, waiting for transfers between devices: 174 us -> none  [per_device(): slab = lax.all_gather(lighting, 'pcol', axis=0, tiled=True)]
    another operation x0 -> x2, local copies, waits for them, and re-layouts: none -> 18.6 us  [the longest x1 17.2 us: per_device(): slab_flat = slab.reshape(slab_count, tile_size * col_width)]
    reshape x1 -> x0, local copies, waits for them, and re-layouts: 17.2 us -> none  [per_device(): slab_flat = slab.reshape(slab_count, tile_size * col_width)]
    ppermute x0 -> x7, starting transfers between devices: none -> 17.2 us  [the longest x3 9.15 us: target_pass(): ppermute(everything[-1] if everything else field, axis_name=device_axis,...]
    unnamed x7 -> x24, local copies, waits for them, and re-layouts: 1.58 us -> 18.2 us
    gather x0 -> x1, local copies, waits for them, and re-layouts: none -> 11.4 us  [target_pass(): plain = plain[(jnp.arange(p_count) - newest) % p_count]]
  transfers between devices with their start and end apart: 3 -> 9, of which waited for: 2 -> 5; matrix products, arithmetic and copies ran while one was open for 72% -> 69% of each run, Pallas kernels for 0% -> 0%
where the time goes in v1:
time: 887 us; the launch traced here: 885 us
  local copies, waits for them, and re-layouts  449 us (51%)
  waiting for transfers between devices  238 us (27%)
  matrix products  154 us (17%)
  starting transfers between devices  25.2 us (3%)
  other arithmetic  17.8 us (2%)
    ppermute x4, waiting for transfers between devices, target_pass(): ppermute(current_block[-1] if current_block else field, axis_name=device_...  222 us
    while x20, local copies, waits for them, and re-layouts  205 us
    gather x10, local copies, waits for them, and re-layouts, one_group(): jnp.take(slab_flat, col_set, axis=0)  186 us
    dot_general x10, matrix products, one_group(): jnp.einsum('gpq,gqk->gpk', block_set, picked, preferred_element_type=jnp....  78.9 us
    dot_general x10, matrix products, one_group(): jnp.dot(placing, product.reshape(group_size, tile_size * col_width), prec...  74.1 us
    unnamed x24, local copies, waits for them, and re-layouts  18.2 us
  transfers between devices with their start and end apart: 9, of which 5 were waited for; matrix products, arithmetic and copies ran while one was open for 69% of the time, Pallas kernels for 0%

profile of v1, /device:TPU:0, one launch (start us, length us, event | category | flops | bytes accessed | tf_op | source)
XLA Modules:
  0.0 885.1 jit_solution(713574305366551290)
XLA Ops:
  3.0 37.6 %collective-permute-done = bf16[2048,384]{1,0:T(8,128)(2,1)S(1)} collective-permute-done((bf16[2048,384]{1,0:T(8,128)(2,1)}, bf16[2048,384]{1,0:T(8,128)(2,1)S(1)}, u32[]{:S(2)}, u32[]{:S(2)}) %collective-permute-start) | collective-permute-done | bytes 1572896 | tf_op jit(solution)/shard_map/ppermute | solution.py:23
  46.5 62.4 %collective-permute-done.1 = bf16[2048,384]{1,0:T(8,128)(2,1)S(1)} collective-permute-done((bf16[2048,384]{1,0:T(8,128)(2,1)S(1)}, bf16[2048,384]{1,0:T(8,128)(2,1)S(1)}, u32[]{:S(2)}, u32[]{:S(2)}) %collective-permute-start.1) | collective-permute-done | bytes 1572896 | tf_op jit(solution)/shard_map/ppermute | solution.py:23
  114.7 63.9 %collective-permute-done.2 = bf16[2048,384]{1,0:T(8,128)(2,1)} collective-permute-done((bf16[2048,384]{1,0:T(8,128)(2,1)S(1)}, bf16[2048,384]{1,0:T(8,128)(2,1)}, u32[]{:S(2)}, u32[]{:S(2)}) %collective-permute-start.2) | collective-permute-done | bytes 1572896 | tf_op jit(solution)/shard_map/ppermute | solution.py:23
  190.1 57.8 %collective-permute-done.3 = bf16[2048,384]{1,0:T(8,128)(2,1)} collective-permute-done((bf16[2048,384]{1,0:T(8,128)(2,1)}, bf16[2048,384]{1,0:T(8,128)(2,1)}, u32[]{:S(2)}, u32[]{:S(2)}) %collective-permute-start.3) | collective-permute-done | bytes 1572896 | tf_op jit(solution)/shard_map/ppermute | solution.py:23
  275.5 17.2 %reshape_reshape.3 = bf16[128,49152]{1,0:T(8,128)(2,1)} reshape(bf16[8,2048,384]{2,1,0:T(8,128)(2,1)} %gather_fusion.1) | data formatting | bytes 25165824 | tf_op jit(solution)/shard_map/reshape;reshape | solution.py:51
  292.8 558.7 %while.11 = (s32[]{:T(128)}, f32[16,49152]{1,0:T(8,128)S(1)}, s32[10,64]{1,0:T(8,128)S(1)}, bf16[10,64,128,128]{3,2,1,0:T(8,128)(2,1)}, s32[10,64]{1,0:T(8,128)S...) while((s32[]{:T(128)}, f32[16,49152]{1,0:T(8,128)S(1)}, s32[10,64]{1,0:T(8,128)S(1)}, ...), condition=%wide.region_2.3_spmd.clone, body=%wide.region_1.2_spmd.clone.sunk | while | flops 1414007296 | bytes 102767336 | solution.py:72
  292.8 18.6 %gather_fusion = bf16[64,49152]{1,0:T(8,128)(2,1)} fusion(bf16[128,49152]{1,0:T(8,128)(2,1)} %get-tuple-element.136, s32[1024]{0:T(1024)S(1)} %pad_clamp_fusion.3), kind=kCustom, calls=%fused_computation.clone.clone.1 | custom fusion | bytes 12583168 | tf_op jit(solution)/shard_map/while/body/eval_jaxpr/jit(_take)/gather | solution.py:60
  324.9 16.3 %copy.33 = f32[8,8,128,384]{3,1,2,0:T(8,128)} copy(f32[8,8,128,384]{3,2,1,0:T(8,128)} %bitcast.77) | data formatting | bytes 25165824 | tf_op jit(solution)/shard_map/while
  348.6 18.6 %gather_fusion = bf16[64,49152]{1,0:T(8,128)(2,1)} fusion(bf16[128,49152]{1,0:T(8,128)(2,1)} %get-tuple-element.136, s32[1024]{0:T(1024)S(1)} %pad_clamp_fusion.3), kind=kCustom, calls=%fused_computation.clone.clone.1 | custom fusion | bytes 12583168 | tf_op jit(solution)/shard_map/while/body/eval_jaxpr/jit(_take)/gather | solution.py:60
  380.8 16.3 %copy.33 = f32[8,8,128,384]{3,1,2,0:T(8,128)} copy(f32[8,8,128,384]{3,2,1,0:T(8,128)} %bitcast.77) | data formatting | bytes 25165824 | tf_op jit(solution)/shard_map/while
  404.5 18.6 %gather_fusion = bf16[64,49152]{1,0:T(8,128)(2,1)} fusion(bf16[128,49152]{1,0:T(8,128)(2,1)} %get-tuple-element.136, s32[1024]{0:T(1024)S(1)} %pad_clamp_fusion.3), kind=kCustom, calls=%fused_computation.clone.clone.1 | custom fusion | bytes 12583168 | tf_op jit(solution)/shard_map/while/body/eval_jaxpr/jit(_take)/gather | solution.py:60
  436.6 16.3 %copy.33 = f32[8,8,128,384]{3,1,2,0:T(8,128)} copy(f32[8,8,128,384]{3,2,1,0:T(8,128)} %bitcast.77) | data formatting | bytes 25165824 | tf_op jit(solution)/shard_map/while
  460.3 18.6 %gather_fusion = bf16[64,49152]{1,0:T(8,128)(2,1)} fusion(bf16[128,49152]{1,0:T(8,128)(2,1)} %get-tuple-element.136, s32[1024]{0:T(1024)S(1)} %pad_clamp_fusion.3), kind=kCustom, calls=%fused_computation.clone.clone.1 | custom fusion | bytes 12583168 | tf_op jit(solution)/shard_map/while/body/eval_jaxpr/jit(_take)/gather | solution.py:60
  492.5 16.3 %copy.33 = f32[8,8,128,384]{3,1,2,0:T(8,128)} copy(f32[8,8,128,384]{3,2,1,0:T(8,128)} %bitcast.77) | data formatting | bytes 25165824 | tf_op jit(solution)/shard_map/while
  516.2 18.6 %gather_fusion = bf16[64,49152]{1,0:T(8,128)(2,1)} fusion(bf16[128,49152]{1,0:T(8,128)(2,1)} %get-tuple-element.136, s32[1024]{0:T(1024)S(1)} %pad_clamp_fusion.3), kind=kCustom, calls=%fused_computation.clone.clone.1 | custom fusion | bytes 12583168 | tf_op jit(solution)/shard_map/while/body/eval_jaxpr/jit(_take)/gather | solution.py:60
  548.3 16.3 %copy.33 = f32[8,8,128,384]{3,1,2,0:T(8,128)} copy(f32[8,8,128,384]{3,2,1,0:T(8,128)} %bitcast.77) | data formatting | bytes 25165824 | tf_op jit(solution)/shard_map/while
  572.0 18.6 %gather_fusion = bf16[64,49152]{1,0:T(8,128)(2,1)} fusion(bf16[128,49152]{1,0:T(8,128)(2,1)} %get-tuple-element.136, s32[1024]{0:T(1024)S(1)} %pad_clamp_fusion.3), kind=kCustom, calls=%fused_computation.clone.clone.1 | custom fusion | bytes 12583168 | tf_op jit(solution)/shard_map/while/body/eval_jaxpr/jit(_take)/gather | solution.py:60
  604.2 16.3 %copy.33 = f32[8,8,128,384]{3,1,2,0:T(8,128)} copy(f32[8,8,128,384]{3,2,1,0:T(8,128)} %bitcast.77) | data formatting | bytes 25165824 | tf_op jit(solution)/shard_map/while
  627.9 18.6 %gather_fusion = bf16[64,49152]{1,0:T(8,128)(2,1)} fusion(bf16[128,49152]{1,0:T(8,128)(2,1)} %get-tuple-element.136, s32[1024]{0:T(1024)S(1)} %pad_clamp_fusion.3), kind=kCustom, calls=%fused_computation.clone.clone.1 | custom fusion | bytes 12583168 | tf_op jit(solution)/shard_map/while/body/eval_jaxpr/jit(_take)/gather | solution.py:60
  660.0 16.3 %copy.33 = f32[8,8,128,384]{3,1,2,0:T(8,128)} copy(f32[8,8,128,384]{3,2,1,0:T(8,128)} %bitcast.77) | data formatting | bytes 25165824 | tf_op jit(solution)/shard_map/while
  683.8 18.6 %gather_fusion = bf16[64,49152]{1,0:T(8,128)(2,1)} fusion(bf16[128,49152]{1,0:T(8,128)(2,1)} %get-tuple-element.136, s32[1024]{0:T(1024)S(1)} %pad_clamp_fusion.3), kind=kCustom, calls=%fused_computation.clone.clone.1 | custom fusion | bytes 12583168 | tf_op jit(solution)/shard_map/while/body/eval_jaxpr/jit(_take)/gather | solution.py:60
  739.6 18.6 %gather_fusion = bf16[64,49152]{1,0:T(8,128)(2,1)} fusion(bf16[128,49152]{1,0:T(8,128)(2,1)} %get-tuple-element.136, s32[1024]{0:T(1024)S(1)} %pad_clamp_fusion.3), kind=kCustom, calls=%fused_computation.clone.clone.1 | custom fusion | bytes 12583168 | tf_op jit(solution)/shard_map/while/body/eval_jaxpr/jit(_take)/gather | solution.py:60
  795.5 18.6 %gather_fusion = bf16[64,49152]{1,0:T(8,128)(2,1)} fusion(bf16[128,49152]{1,0:T(8,128)(2,1)} %get-tuple-element.136, s32[1024]{0:T(1024)S(1)} %pad_clamp_fusion.3), kind=kCustom, calls=%fused_computation.clone.clone.1 | custom fusion | bytes 12583168 | tf_op jit(solution)/shard_map/while/body/eval_jaxpr/jit(_take)/gather | solution.py:60
  862.1 16.6 %all-to-all-done.1 = bf16[4,4,128,384]{3,1,2,0:T(4,128)(2,1)} async-done(((bf16[4,4,128,384]{3,1,2,0:T(4,128)(2,1)}), bf16[4,4,128,384]{3,1,2,0:T(4,128)(2,1)}, u32[]{:S(2)}, u32[]{:S(2)}) %all-to-all-start.1) | async-done | bytes 1572896 | tf_op jit(solution)/shard_map/all_to_all | solution.py:84
  (141 shorter events, 328.3 us)
Async XLA Ops:
  0.0 40.6 %collective-permute-start = (bf16[2048,384]{1,0:T(8,128)(2,1)}, bf16[2048,384]{1,0:T(8,128)(2,1)S(1)}, u32[]{:S(2)}, u32[]{:S(2)}) collective-permute-start(bf16[2048,384]{1,0:T(8,128)(2,1)} %param.13), channel_id=1, source_target_pairs={{0,1},{1,2},{2,3},{3,4},{4,5},{5,6},{6,7},{7,0},{8,9},{9,10},{10,1... | collective-permute-start | bytes 4718600 | tf_op jit(solution)/shard_map/ppermute | solution.py:23
  40.6 1.1 copy-start.3
  41.7 67.1 %collective-permute-start.1 = (bf16[2048,384]{1,0:T(8,128)(2,1)S(1)}, bf16[2048,384]{1,0:T(8,128)(2,1)S(1)}, u32[]{:S(2)}, u32[]{:S(2)}) collective-permute-start(bf16[2048,384]{1,0:T(8,128)(2,1)S(1)} %collective-permute-done), channel_id=1, source_target_pairs={{0,1},{1,2},{2,3},{3,4},{4,5},{5,6},{6,7},{7,0},{8,9},{9,10},{10,1... | collective-permute-start | bytes 4718600 | tf_op jit(solution)/shard_map/ppermute | solution.py:23
  41.7 70.7 %collective-permute-start.4 = (bf16[2048,384]{1,0:T(8,128)(2,1)}, bf16[2048,384]{1,0:T(8,128)(2,1)}, u32[]{:S(2)}, u32[]{:S(2)}) collective-permute-start(bf16[2048,384]{1,0:T(8,128)(2,1)} %param.13), channel_id=1, source_target_pairs={{1,0},{2,1},{3,2},{4,3},{5,4},{6,5},{7,6},{0,7},{9,8},{10,9},{11,1... | collective-permute-start | bytes 4718600 | tf_op jit(solution)/shard_map/ppermute | solution.py:29
  108.8 1.1 copy-start.5
  110.0 68.7 %collective-permute-start.2 = (bf16[2048,384]{1,0:T(8,128)(2,1)S(1)}, bf16[2048,384]{1,0:T(8,128)(2,1)}, u32[]{:S(2)}, u32[]{:S(2)}) collective-permute-start(bf16[2048,384]{1,0:T(8,128)(2,1)S(1)} %collective-permute-done.1), channel_id=1, source_target_pairs={{0,1},{1,2},{2,3},{3,4},{4,5},{5,6},{6,7},{7,0},{8,9},{9,10},{10,1... | collective-permute-start | bytes 4718600 | tf_op jit(solution)/shard_map/ppermute | solution.py:23
  112.5 75.5 %collective-permute-start.5 = (bf16[2048,384]{1,0:T(8,128)(2,1)}, bf16[2048,384]{1,0:T(8,128)(2,1)}, u32[]{:S(2)}, u32[]{:S(2)}) collective-permute-start(bf16[2048,384]{1,0:T(8,128)(2,1)} %collective-permute-done.4), channel_id=1, source_target_pairs={{1,0},{2,1},{3,2},{4,3},{5,4},{6,5},{7,6},{0,7},{9,8},{10,9},{11,1... | collective-permute-start | bytes 4718600 | tf_op jit(solution)/shard_map/ppermute | solution.py:29
  178.6 69.3 %collective-permute-start.3 = (bf16[2048,384]{1,0:T(8,128)(2,1)}, bf16[2048,384]{1,0:T(8,128)(2,1)}, u32[]{:S(2)}, u32[]{:S(2)}) collective-permute-start(bf16[2048,384]{1,0:T(8,128)(2,1)} %collective-permute-done.2), channel_id=1, source_target_pairs={{0,1},{1,2},{2,3},{3,4},{4,5},{5,6},{6,7},{7,0},{8,9},{9,10},{10,1... | collective-permute-start | bytes 4718600 | tf_op jit(solution)/shard_map/ppermute | solution.py:23
  182.5 671.8 %all-to-all-start = ((s32[4,1,4]{2,1,0:T(1,128)}), s32[4,1,4]{2,1,0:T(1,128)}, u32[]{:S(2)}, u32[]{:S(2)}) async-start(s32[4,1,4]{2,1,0:T(1,128)} %bitcast), calls=%async_computation | async-start | bytes 4096 | tf_op jit(solution)/shard_map/all_to_all | solution.py:91
  187.9 65.5 %copy-start.6 = (bf16[2048,384]{1,0:T(8,128)(2,1)S(1)}, bf16[2048,384]{1,0:T(8,128)(2,1)}, u32[]{:S(2)}) copy-start(bf16[2048,384]{1,0:T(8,128)(2,1)} %copy-done.5) | copy-start | bytes 4718596
  187.9 66.8 %copy-start.4 = (bf16[2048,384]{1,0:T(8,128)(2,1)S(1)}, bf16[2048,384]{1,0:T(8,128)(2,1)}, u32[]{:S(2)}) copy-start(bf16[2048,384]{1,0:T(8,128)(2,1)} %copy-done.3) | copy-start | bytes 4718596
  187.9 68.1 %copy-start.2 = (bf16[2048,384]{1,0:T(8,128)(2,1)S(1)}, bf16[2048,384]{1,0:T(8,128)(2,1)}, u32[]{:S(2)}) copy-start(bf16[2048,384]{1,0:T(8,128)(2,1)} %param.13) | copy-start | bytes 4718596
  187.9 74.9 %collective-permute-start.6 = (bf16[2048,384]{1,0:T(8,128)(2,1)}, bf16[2048,384]{1,0:T(8,128)(2,1)S(1)}, u32[]{:S(2)}, u32[]{:S(2)}) collective-permute-start(bf16[2048,384]{1,0:T(8,128)(2,1)} %collective-permute-done.5), channel_id=1, source_target_pairs={{1,0},{2,1},{3,2},{4,3},{5,4},{6,5},{7,6},{0,7},{9,8},{10,9},{11,1... | collective-permute-start | bytes 4718600 | tf_op jit(solution)/shard_map/ppermute | solution.py:29
  851.5 7.2 copy-start.7
  854.3 24.5 %all-to-all-start.1 = ((bf16[4,4,128,384]{3,1,2,0:T(4,128)(2,1)}), bf16[4,4,128,384]{3,1,2,0:T(4,128)(2,1)}, u32[]{:S(2)}, u32[]{:S(2)}) async-start(bf16[4,4,128,384]{3,1,2,0:T(4,128)(2,1)} %copy.23), calls=%async_computation.1 | async-start | bytes 3145728 | tf_op jit(solution)/shard_map/all_to_all | solution.py:84
  881.2 1.9 copy-start
  881.2 2.3 copy-start.1
